TPU v7x, 512 devices: a whole 4x4x16 slice. The times are simulated.
512 devices in a mesh: dp: 8 (over x, z_hi), ctx: 64 (over y, z_lo, core).
Axes of the slice: x: 4, y: 4, z: 16 (z_hi: 2, z_lo: 8; z = z_hi * 8 + z_lo), core: 2. Of those that a mesh axis runs over, the one named last changes fastest.
Arguments:
- inputs: float32 [8, 2048, 8192], P('dp', None, 'ctx'), may hold values from -6 to 6
- grad_out: float32 [8, 2048, 8192], P('dp', None, 'ctx'), may hold values from -6 to 6
- filters: float32 [2048, 8192], P(('dp', 'ctx')), may hold values from -0.0625 to 0.0625
Outputs:
- input_grad: float32 [8, 2048, 8192], P('dp', None, 'ctx')
- filter_grad: float32 [2048, 8192], P(('dp', 'ctx'))
All inputs are finite; a program needn't handle non-finite values.
Results may differ from a plain program's by a relative error of at most 0.000098.
Values sent between devices are 32-bit elements; how exact they have to be, the bound alone decides.
No kernel may reach another device: no remote copies, remote signals or barrier semaphores. Data moves between devices by JAX's collectives and lax.ppermute only.
A program may use at most 64 MiB of HBM per device.

v0:
```python
import math
import jax
import jax.numpy as jnp
from jax import lax
from jax.sharding import PartitionSpec as P


def dft_tables(seq_length):
    inner_size = 128
    padded_size = 2 * seq_length
    outer_size = padded_size // inner_size
    signal_rows = seq_length // inner_size
    freq_count = outer_size // 2 + 1
    two_pi = 2.0 * math.pi
    order_rows = jnp.arange(signal_rows, dtype=jnp.int32)
    order_freq = jnp.arange(freq_count, dtype=jnp.int32)
    order_inner = jnp.arange(inner_size, dtype=jnp.int32)
    angle_outer = (
        two_pi
        / outer_size
        * (order_rows[:, None] * order_freq[None, :] % outer_size).astype(jnp.float32)
    )
    cos_outer = jnp.cos(angle_outer)
    sin_outer = jnp.sin(angle_outer)
    first_table = jnp.concatenate([cos_outer, -sin_outer], axis=1)
    weights = jnp.where((order_freq == 0) | (order_freq == freq_count - 1), 1.0, 2.0).astype(
        jnp.float32
    )
    last_table = jnp.concatenate(
        [(cos_outer * weights[None, :]).T, (-sin_outer * weights[None, :]).T], axis=0
    )
    angle_inner = (
        two_pi
        / inner_size
        * (order_inner[:, None] * order_inner[None, :] % inner_size).astype(jnp.float32)
    )
    cos_inner = jnp.cos(angle_inner)
    sin_inner = jnp.sin(angle_inner)
    forward_block = jnp.concatenate(
        [
            jnp.concatenate([cos_inner, -sin_inner], axis=1),
            jnp.concatenate([sin_inner, cos_inner], axis=1),
        ],
        axis=0,
    )
    inverse_block = jnp.concatenate(
        [
            jnp.concatenate([cos_inner, sin_inner], axis=1),
            jnp.concatenate([-sin_inner, cos_inner], axis=1),
        ],
        axis=0,
    )
    angle_turn = (
        two_pi
        / padded_size
        * (order_freq[:, None] * order_inner[None, :] % padded_size).astype(jnp.float32)
    )
    return (
        first_table,
        last_table,
        forward_block,
        inverse_block,
        jnp.cos(angle_turn),
        jnp.sin(angle_turn),
        freq_count,
        signal_rows,
        padded_size,
    )


def forward_spectrum(signal, tables):
    (
        first_table,
        last_table,
        forward_block,
        inverse_block,
        cos_turn,
        sin_turn,
        freq_count,
        signal_rows,
        padded_size,
    ) = tables
    highest = lax.Precision.HIGHEST
    row_count = signal.shape[0]
    shaped = signal.reshape(row_count, signal_rows, 128)
    first = jnp.einsum("man,ak->mkn", shaped, first_table, precision=highest)
    first_real = first[:, :freq_count]
    first_imag = first[:, freq_count:]
    turned = jnp.concatenate(
        [
            first_real * cos_turn + first_imag * sin_turn,
            first_imag * cos_turn - first_real * sin_turn,
        ],
        axis=-1,
    )
    return jnp.einsum("mkn,nj->mkj", turned, forward_block, precision=highest)


def inverse_signal(spec_real, spec_imag, tables):
    (
        first_table,
        last_table,
        forward_block,
        inverse_block,
        cos_turn,
        sin_turn,
        freq_count,
        signal_rows,
        padded_size,
    ) = tables
    highest = lax.Precision.HIGHEST
    row_count = spec_real.shape[0]
    stacked = jnp.concatenate([spec_real, spec_imag], axis=-1)
    middle = jnp.einsum("mkj,jn->mkn", stacked, inverse_block, precision=highest)
    middle_real = middle[..., :128]
    middle_imag = middle[..., 128:]
    back = jnp.concatenate(
        [
            middle_real * cos_turn - middle_imag * sin_turn,
            middle_imag * cos_turn + middle_real * sin_turn,
        ],
        axis=1,
    )
    result = jnp.einsum("mkn,ka->man", back, last_table, precision=highest)
    return (result / padded_size).reshape(row_count, -1)


def shards(inputs, grad_out, filters):
    dp_count = lax.axis_size("dp")
    ctx_count = lax.axis_size("ctx")
    seq_local, channel_count, local_tokens = inputs.shape
    owned_channels = channel_count // (dp_count * ctx_count)
    seq_length = local_tokens * ctx_count
    tables = dft_tables(seq_length)
    freq_count = tables[6]
    split_shape = (seq_local, dp_count, ctx_count, owned_channels, local_tokens)
    split_input = inputs.reshape(split_shape)
    split_grad = grad_out.reshape(split_shape)
    norm_factor = 1.0 / math.sqrt(seq_local * dp_count * seq_length)
    moved_input, moved_grad = (
        lax.all_to_all(split_input, "ctx", split_axis=2, concat_axis=4, tiled=True),
        lax.all_to_all(split_grad, "ctx", split_axis=2, concat_axis=4, tiled=True),
    )
    channels = dp_count * owned_channels
    filter_rows = lax.all_gather(filters, "dp", axis=0, tiled=True)
    spec_shape = (seq_local, channels, freq_count, 256)
    input_spec = forward_spectrum(
        moved_input.reshape(seq_local * channels, seq_length), tables
    ).reshape(spec_shape)
    grad_spec = forward_spectrum(
        moved_grad.reshape(seq_local * channels, seq_length), tables
    ).reshape(spec_shape)
    filter_spec = forward_spectrum(filter_rows, tables)[None]
    input_real = input_spec[..., :128]
    input_imag = input_spec[..., 128:]
    grad_real = grad_spec[..., :128]
    grad_imag = grad_spec[..., 128:]
    filter_real = filter_spec[..., :128]
    filter_imag = filter_spec[..., 128:]
    product_real = grad_real * filter_real + grad_imag * filter_imag
    product_imag = grad_imag * filter_real - grad_real * filter_imag
    input_part = inverse_signal(
        product_real.reshape(seq_local * channels, freq_count, 128),
        product_imag.reshape(seq_local * channels, freq_count, 128),
        tables,
    )
    corr_real = jnp.sum(grad_real * input_real + grad_imag * input_imag, axis=0)
    corr_imag = jnp.sum(grad_imag * input_real - grad_real * input_imag, axis=0)
    filter_part = inverse_signal(corr_real, corr_imag, tables) * norm_factor
    leaving = input_part.reshape(seq_local, dp_count, 1, owned_channels, seq_length)
    returned = lax.all_to_all(leaving, "ctx", split_axis=4, concat_axis=2, tiled=True)
    summed = lax.psum_scatter(
        filter_part.reshape(dp_count, owned_channels, seq_length),
        "dp",
        scatter_dimension=0,
        tiled=True,
    )
    filter_grad = summed.reshape(owned_channels, seq_length)
    input_grad = returned.reshape(seq_local, channel_count, local_tokens)
    return (input_grad, filter_grad)


def solution(mesh):
    placed = (P("dp", None, "ctx"), P("dp", None, "ctx"), P(("dp", "ctx"), None))
    return jax.shard_map(
        shards,
        mesh=mesh,
        in_specs=placed,
        out_specs=(P("dp", None, "ctx"), P(("dp", "ctx"), None)),
        check_vma=False,
    )
```

profile of v0, /device:TPU:14, one launch (start us, length us, event | category | flops | bytes accessed | tf_op | source)
XLA Modules:
  0.0 565.3 jit_solution(7946573195563729075)
XLA Ops:
  7.2 2.5 copy.18
  9.7 16.3 %all-to-all-start = ((f32[1,8,64,4,128]{4,3,1,0,2:T(4,128)}), f32[1,8,64,4,128]{4,3,1,0,2:T(4,128)S(1)}, u32[]{:S(2)}, u32[]{:S(2)}) async-start(f32[1,8,64,4,128]{4,3,1,0,2:T(4,128)} %copy.18), calls=%async_computation | async-start | bytes 2097152 | tf_op jit(solution)/shard_map/all_to_all | solution.py:142
  26.0 1.3 copy.22
  27.3 49.3 %all-to-all-done = f32[1,8,64,4,128]{4,3,1,0,2:T(4,128)S(1)} async-done(((f32[1,8,64,4,128]{4,3,1,0,2:T(4,128)}), f32[1,8,64,4,128]{4,3,1,0,2:T(4,128)S(1)}, u32[]{:S(2)}, u32[]{:S(2)}) %all-to-all-start) | async-done | bytes 1048608 | tf_op jit(solution)/shard_map/all_to_all | solution.py:142
  76.6 9.0 %all-to-all-start.2 = ((f32[1,8,64,4,128]{4,3,1,0,2:T(4,128)}), f32[1,8,64,4,128]{4,3,1,0,2:T(4,128)}, u32[]{:S(2)}, u32[]{:S(2)}) async-start(f32[1,8,64,4,128]{4,3,1,0,2:T(4,128)} %copy.22), calls=%async_computation.2 | async-start | bytes 2097152 | tf_op jit(solution)/shard_map/all_to_all | solution.py:141
  86.8 0.8 fusion.85
  87.9 0.8 cosine_multiply_fusion
  88.7 99.1 %all-gather.3.cloned.1.call-done = f32[8,4,8192]{2,1,0:T(4,128)} async-done(((f32[1,4,8192]{2,1,0:T(4,128)}), f32[8,4,8192]{2,1,0:T(4,128)}) %all-gather.3.cloned.1.call-update) | async-done | bytes 1048592 | tf_op jit(solution)/shard_map/all_gather | solution.py:145
  187.7 1.9 reshape.87
  189.7 2.0 convolution_bitcast_fusion.1
  192.3 3.4 convolution_bitcast_fusion.2
  195.7 1.8 copy.23
  197.6 2.0 convolution_bitcast_fusion
  199.6 0.9 multiply_add_fusion.1
  200.6 2.6 fusion.31
  203.1 2.1 fusion.34
  205.2 2.1 fusion.28
  208.1 2.1 fusion.8
  210.2 2.1 fusion.16
  213.1 2.4 fusion.46
  215.5 1.6 reshape_reshape.10
  217.2 10.7 %copy.20 = f32[1,8,1,4,8192]{1,3,2,0,4:T(4,128)} copy(f32[1,8,1,4,8192]{4,3,1,2,0:T(4,128)S(1)} %reshape_reshape.10) | data formatting | bytes 2097152 | tf_op jit(solution)/shard_map/reshape;reshape | solution.py:170
  227.9 22.0 %reshape.102 = f32[64,1,4096]{2,1,0:T(1,128)} reshape(f32[8192,1,1,4,8]{4,3,2,1,0:T(4,128)} %bitcast.65) | data formatting | bytes 2097152
  249.8 5.8 %all-to-all-start.1 = ((f32[64,1,4096]{2,1,0:T(1,128)}), f32[64,1,4096]{2,1,0:T(1,128)S(1)}, u32[]{:S(2)}, u32[]{:S(2)}) async-start(f32[64,1,4096]{2,1,0:T(1,128)} %reshape.102), calls=%async_computation.1 | async-start | bytes 2097152 | tf_op jit(solution)/shard_map/all_to_all | solution.py:171
  255.6 2.4 fusion.40
  258.1 2.6 mul.580
  260.7 1.3 dynamic-slice
  262.1 256.1 %all-reduce.3.cloned.1.call-done = f32[8,4,8192]{2,1,0:T(4,128)} async-done(((f32[8,4,8192]{2,1,0:T(4,128)}), f32[8,4,8192]{2,1,0:T(4,128)}) %all-reduce.3.cloned.1.call-update) | async-done | bytes 1048592
  518.1 2.2 dynamic-slice_bitcast_fusion
  520.8 3.3 reduce
  524.1 21.2 %reshape.103 = f32[8192,1,1,4,8]{4,3,2,1,0:T(4,128)} reshape(f32[64,4096]{1,0:T(8,128)S(1)} %reduce) | data formatting | bytes 2097152
  545.3 13.0 %copy.21 = f32[1,8,64,1,4,128]{5,4,2,1,3,0:T(4,128)} copy(f32[1,8,64,1,4,128]{1,4,5,2,3,0:T(4,128)} %bitcast.66) | data formatting | bytes 2097152 | tf_op jit(solution)/shard_map/all_to_all | solution.py:171
  (30 shorter events, 4.1 us)
Async XLA Ops:
  9.7 16.3 %copy-start.3 = (f32[1,2048,128]{2,1,0:T(8,128)S(1)}, f32[1,2048,128]{2,1,0:T(8,128)}, u32[]{:S(2)}) copy-start(f32[1,2048,128]{2,1,0:T(8,128)} %param.3) | copy-start | bytes 3145732
  9.7 66.9 %all-to-all-start = ((f32[1,8,64,4,128]{4,3,1,0,2:T(4,128)}), f32[1,8,64,4,128]{4,3,1,0,2:T(4,128)S(1)}, u32[]{:S(2)}, u32[]{:S(2)}) async-start(f32[1,8,64,4,128]{4,3,1,0,2:T(4,128)} %copy.18), calls=%async_computation | async-start | bytes 2097152 | tf_op jit(solution)/shard_map/all_to_all | solution.py:142
  76.6 10.2 %copy-start.1 = (f32[1,8,64,4,128]{4,3,1,0,2:T(4,128)}, f32[1,8,64,4,128]{4,3,1,0,2:T(4,128)S(1)}, u32[]{:S(2)}) copy-start(f32[1,8,64,4,128]{4,3,1,0,2:T(4,128)S(1)} %all-to-all-done) | copy-start | bytes 3145732
  76.6 119.1 %all-to-all-start.2 = ((f32[1,8,64,4,128]{4,3,1,0,2:T(4,128)}), f32[1,8,64,4,128]{4,3,1,0,2:T(4,128)}, u32[]{:S(2)}, u32[]{:S(2)}) async-start(f32[1,8,64,4,128]{4,3,1,0,2:T(4,128)} %copy.22), calls=%async_computation.2 | async-start | bytes 2097152 | tf_op jit(solution)/shard_map/all_to_all | solution.py:141
  85.6 102.1 %all-gather.3.cloned.1.call-start = ((), (), s32[]{:S(2)}) async-start(), calls=%async_computation.3 | async-start | bytes 1179648 | tf_op jit(solution)/shard_map/all_gather | solution.py:145
  189.7 2.0 copy-start.2
  197.6 2.1 copy-start
  197.6 2.1 copy-start.4
  197.6 2.1 copy-start.5
  212.3 0.8 copy-start.6
  212.3 0.8 copy-start.7
  249.8 270.5 %all-to-all-start.1 = ((f32[64,1,4096]{2,1,0:T(1,128)}), f32[64,1,4096]{2,1,0:T(1,128)S(1)}, u32[]{:S(2)}, u32[]{:S(2)}) async-start(f32[64,1,4096]{2,1,0:T(1,128)} %reshape.102), calls=%async_computation.1 | async-start | bytes 2097152 | tf_op jit(solution)/shard_map/all_to_all | solution.py:171
  255.6 262.5 %all-reduce.3.cloned.1.call-start = ((), (), s32[]{:S(2)}) async-start(), calls=%async_computation.4 | async-start | bytes 2097152
Sparse Core Ops, SparseCore 0:
  89.7 97.9 all-gather.2
  260.9 257.2 all-reduce.2
where the time goes:
time: 569 us; the launch traced here: 565 us
  waiting for transfers between devices  405 us (71%)
  local copies, waits for them, and re-layouts  83.6 us (15%)
  starting transfers between devices  31.4 us (6%)
  matrix products  23.2 us (4%)
  between operations  14.5 us (3%)
  other arithmetic  7.71 us (1%)
    unnamed x3, waiting for transfers between devices  256 us
    all_gather x1, waiting for transfers between devices, shards(): filter_rows = lax.all_gather(filters, 'dp', axis=0, tiled=True)  99.1 us
    all_to_all x1, waiting for transfers between devices, shards(): lax.all_to_all(split_grad, 'ctx', split_axis=2, concat_axis=4, tiled=True)  49.3 us
    unnamed x19, local copies, waits for them, and re-layouts  44.8 us
    all_to_all x1, starting transfers between devices, shards(): lax.all_to_all(split_grad, 'ctx', split_axis=2, concat_axis=4, tiled=True)  16.3 us
    all_to_all x2, local copies, waits for them, and re-layouts, shards(): lax.all_to_all(leaving, 'ctx', split_axis=4, concat_axis=2, tiled=True)  13.5 us
    another operation x2, local copies, waits for them, and re-layouts, shards(): input_part.reshape(seq_local, dp_count, 1, owned_channels, seq_length)  12.3 us
  transfers between devices with their start and end apart: 5, of which 3 were waited for; matrix products, arithmetic and copies ran while one was open for 4% of the time, Pallas kernels for 0%

commit v1 on v0

--- a/solution.py
+++ b/solution.py
@@ -168,7 +168,9 @@
     corr_imag = jnp.sum(grad_imag * input_real - grad_real * input_imag, axis=0)
     filter_part = inverse_signal(corr_real, corr_imag, tables) * norm_factor
     leaving = input_part.reshape(seq_local, dp_count, 1, owned_channels, seq_length)
-    returned = lax.all_to_all(leaving, "ctx", split_axis=4, concat_axis=2, tiled=True)
+    cells = jnp.split(leaving, lax.axis_size("ctx"), axis=4)
+    received = lax.all_to_all(jnp.stack(cells), "ctx", 0, 0)
+    returned = jnp.concatenate(received, axis=2)
     summed = lax.psum_scatter(
         filter_part.reshape(dp_count, owned_channels, seq_length),
         "dp",

time: 569 us -> 582 us (1.023)
  local copies, waits for them, and re-layouts: 83.6 us -> 101 us
    unnamed x19 -> x80, local copies, waits for them, and re-layouts: 44.8 us -> 84.5 us
    all_to_all x2 -> x0, local copies, waits for them, and re-layouts: 13.5 us -> none  [shards(): lax.all_to_all(leaving, 'ctx', split_axis=4, concat_axis=2, tiled=True)]
    another operation x2 -> x1, local copies, waits for them, and re-layouts: 12.3 us -> 1.39 us  [shards(): input_part.reshape(seq_local, dp_count, 1, owned_channels, seq_length)]
  transfers between devices with their start and end apart: 5 -> 5, of which waited for: 3 -> 3; matrix products, arithmetic and copies ran while one was open for 4% -> 3% of each run, Pallas kernels for 0% -> 0%
where the time goes in v1:
time: 582 us; the launch traced here: 578 us
  waiting for transfers between devices  404 us (69%)
  local copies, waits for them, and re-layouts  101 us (17%)
  starting transfers between devices  31.3 us (5%)
  matrix products  22 us (4%)
  between operations  14.3 us (2%)
    unnamed x3, waiting for transfers between devices  256 us
    all_gather x1, waiting for transfers between devices, shards(): filter_rows = lax.all_gather(filters, 'dp', axis=0, tiled=True)  99.1 us
    unnamed x80, local copies, waits for them, and re-layouts  84.5 us
    all_to_all x1, waiting for transfers between devices, shards(): lax.all_to_all(split_grad, 'ctx', split_axis=2, concat_axis=4, tiled=True)  49.3 us
    all_to_all x1, starting transfers between devices, shards(): lax.all_to_all(split_grad, 'ctx', split_axis=2, concat_axis=4, tiled=True)  16.3 us
  transfers between devices with their start and end apart: 5, of which 3 were waited for; matrix products, arithmetic and copies ran while one was open for 3% of the time, Pallas kernels for 0%

profile of v1, /device:TPU:14, one launch (start us, length us, event | category | flops | bytes accessed | tf_op | source)
XLA Modules:
  0.0 577.9 jit_solution(10288572109656154985)
XLA Ops:
  7.2 2.5 copy.11
  9.7 16.3 %all-to-all-start = ((f32[1,8,64,4,128]{4,3,1,0,2:T(4,128)}), f32[1,8,64,4,128]{4,3,1,0,2:T(4,128)S(1)}, u32[]{:S(2)}, u32[]{:S(2)}) async-start(f32[1,8,64,4,128]{4,3,1,0,2:T(4,128)} %copy.11), calls=%async_computation | async-start | bytes 2097152 | tf_op jit(solution)/shard_map/all_to_all | solution.py:142
  27.3 49.3 %all-to-all-done = f32[1,8,64,4,128]{4,3,1,0,2:T(4,128)S(1)} async-done(((f32[1,8,64,4,128]{4,3,1,0,2:T(4,128)}), f32[1,8,64,4,128]{4,3,1,0,2:T(4,128)S(1)}, u32[]{:S(2)}, u32[]{:S(2)}) %all-to-all-start) | async-done | bytes 1048608 | tf_op jit(solution)/shard_map/all_to_all | solution.py:142
  76.6 9.0 %all-to-all-start.2 = ((f32[1,8,64,4,128]{4,3,1,0,2:T(4,128)}), f32[1,8,64,4,128]{4,3,1,0,2:T(4,128)}, u32[]{:S(2)}, u32[]{:S(2)}) async-start(f32[1,8,64,4,128]{4,3,1,0,2:T(4,128)} %copy.14), calls=%async_computation.2 | async-start | bytes 2097152 | tf_op jit(solution)/shard_map/all_to_all | solution.py:141
  88.7 99.1 %all-gather.3.cloned.1.call-done = f32[8,4,8192]{2,1,0:T(4,128)} async-done(((f32[1,4,8192]{2,1,0:T(4,128)}), f32[8,4,8192]{2,1,0:T(4,128)}) %all-gather.3.cloned.1.call-update) | async-done | bytes 1048592 | tf_op jit(solution)/shard_map/all_gather | solution.py:145
  187.7 1.9 reshape.86
  189.7 2.0 convolution_bitcast_fusion.1
  192.3 3.4 convolution_bitcast_fusion.2
  195.7 1.8 copy.15
  197.6 2.0 convolution_bitcast_fusion
  200.6 2.3 fusion.31
  202.9 2.1 fusion.34
  205.0 2.1 fusion.28
  207.9 2.1 fusion.8
  210.0 2.1 fusion.16
  212.8 1.5 fusion.46
  214.3 1.4 reshape_reshape.13
  218.3 1.3 constant_dynamic-update-slice_fusion.61
  222.3 1.3 constant_dynamic-update-slice_fusion.58
  243.4 1.3 constant_dynamic-update-slice_fusion.42
  244.7 1.3 constant_dynamic-update-slice_fusion.41
  255.2 1.3 constant_dynamic-update-slice_fusion.33
  265.8 1.3 constant_dynamic-update-slice_fusion.25
  271.0 1.3 constant_dynamic-update-slice_fusion.21
  281.6 1.3 constant_dynamic-update-slice_fusion.13
  285.5 1.3 constant_dynamic-update-slice_fusion.10
  292.1 1.3 constant_dynamic-update-slice_fusion.5
  300.0 5.8 all-to-all-start.1
  305.8 2.4 fusion.40
  308.3 2.6 mul.580
  312.2 255.5 %all-reduce.3.cloned.1.call-done = f32[8,4,8192]{2,1,0:T(4,128)} async-done(((f32[8,4,8192]{2,1,0:T(4,128)}), f32[8,4,8192]{2,1,0:T(4,128)}) %all-reduce.3.cloned.1.call-update) | async-done | bytes 1048592
  567.7 2.2 dynamic-slice_bitcast_fusion
  (89 shorter events, 80.9 us)
Async XLA Ops:
  9.7 16.3 %copy-start.3 = (f32[1,2048,128]{2,1,0:T(8,128)S(1)}, f32[1,2048,128]{2,1,0:T(8,128)}, u32[]{:S(2)}) copy-start(f32[1,2048,128]{2,1,0:T(8,128)} %param.3) | copy-start | bytes 3145732
  9.7 66.9 %all-to-all-start = ((f32[1,8,64,4,128]{4,3,1,0,2:T(4,128)}), f32[1,8,64,4,128]{4,3,1,0,2:T(4,128)S(1)}, u32[]{:S(2)}, u32[]{:S(2)}) async-start(f32[1,8,64,4,128]{4,3,1,0,2:T(4,128)} %copy.11), calls=%async_computation | async-start | bytes 2097152 | tf_op jit(solution)/shard_map/all_to_all | solution.py:142
  76.6 10.2 %copy-start.1 = (f32[1,8,64,4,128]{4,3,1,0,2:T(4,128)}, f32[1,8,64,4,128]{4,3,1,0,2:T(4,128)S(1)}, u32[]{:S(2)}) copy-start(f32[1,8,64,4,128]{4,3,1,0,2:T(4,128)S(1)} %all-to-all-done) | copy-start | bytes 3145732
  76.6 119.1 %all-to-all-start.2 = ((f32[1,8,64,4,128]{4,3,1,0,2:T(4,128)}), f32[1,8,64,4,128]{4,3,1,0,2:T(4,128)}, u32[]{:S(2)}, u32[]{:S(2)}) async-start(f32[1,8,64,4,128]{4,3,1,0,2:T(4,128)} %copy.14), calls=%async_computation.2 | async-start | bytes 2097152 | tf_op jit(solution)/shard_map/all_to_all | solution.py:141
  85.6 102.1 %all-gather.3.cloned.1.call-start = ((), (), s32[]{:S(2)}) async-start(), calls=%async_computation.3 | async-start | bytes 1179648 | tf_op jit(solution)/shard_map/all_gather | solution.py:145
  189.7 2.0 copy-start.2
  197.6 2.1 copy-start
  197.6 2.1 copy-start.4
  197.6 2.1 copy-start.5
  212.1 0.8 copy-start.6
  212.1 0.8 copy-start.7
  300.0 269.9 %all-to-all-start.1 = ((f32[64,1,8,1,4,128]{5,4,2,3,1,0:T(4,128)}), f32[64,1,8,1,4,128]{5,4,2,3,1,0:T(4,128)S(1)}, u32[]{:S(2)}, u32[]{:S(2)}) async-start(f32[64,1,8,1,4,128]{5,4,2,3,1,0:T(4,128)} %constant_dynamic-update-slice_fusion), calls=%async_computation.1 | async-start | bytes 2097152 | tf_op jit(solution)/shard_map/all_to_all | solution.py:172
  305.8 261.9 %all-reduce.3.cloned.1.call-start = ((), (), s32[]{:S(2)}) async-start(), calls=%async_computation.4 | async-start | bytes 2097152
Sparse Core Ops, SparseCore 0:
  89.7 97.9 all-gather.2
  311.0 256.6 all-reduce.2
